TPU v7x, 128 devices: a whole 4x4x4 slice. The times are simulated.
128 devices in a mesh: users: 8 (over z, x_lo), srow: 4 (over y), scol: 4 (over x_hi, core).
Axes of the slice: x: 4 (x_hi: 2, x_lo: 2; x = x_hi * 2 + x_lo), y: 4, z: 4, core: 2. Of those that a mesh axis runs over, the one named last changes fastest.
Arguments:
- history: bfloat16 [8192, 65536], P('users', ('srow', 'scol')), as said below
- ridge: float32 [65536], replicated, may hold values from 0.2 to 2
- pivot_inverse: float32 [2, 1024, 1024], replicated, as said below
- panel_ids: int32 [2], replicated, may hold values from 0 to 63, as said below
Outputs:
- factor_first: float32 [16, 4096, 1024], P(('srow', 'scol'), 'users')
- factor_second: float32 [16, 4096, 1024], P(('srow', 'scol'), 'users')
Inputs may be any that keep to these rules, and one draw needn't show every extreme that they name: `history`: about a third of the entries are nonzero; users and items have scales spread over a factor of ten. `pivot_inverse`: each matrix has a positive diagonal and small entries off it. `panel_ids`: 2 distinct panel numbers; the last panel is always among them.
All inputs are finite; a program needn't handle non-finite values.
Results may differ from a plain program's by a relative error of at most 0.0003.
Values may be sent and summed in bfloat16 or wider, within the bound.
A program may use at most 192 MiB of HBM per device.

v0:
```python
import functools

import jax
import jax.numpy as jnp
from jax import lax
from jax.experimental import pallas as pl
from jax.experimental.pallas import tpu as pltpu
from jax.sharding import PartitionSpec as P

MESH = pl.DeviceIdType.MESH
F32 = jnp.float32
BF16 = jnp.bfloat16
I16 = jnp.int16

CW = 256
KINDS = "ZZXZXZXZ"
NCH = len(KINDS)
HALF = NCH // 2
ORDER = {k: [c for c in range(NCH) if KINDS[c] == k] for k in "ZX"}
NTH = [ORDER[k].index(c) for c, k in enumerate(KINDS)]
TOP = 32767.0


def encode(v):
    top = jnp.maximum(jnp.max(jnp.abs(v), axis=0, keepdims=True), 1e-30)
    q = jnp.round(v * (TOP / top)).astype(jnp.int32).astype(I16)
    return q, top * (1.0 / TOP)


def decode(q, s):
    return q.astype(jnp.int32).astype(F32) * s


def split(v):
    hi = v.astype(BF16)
    return hi, (v - hi.astype(F32)).astype(BF16)


def dot3(a, b, dims=(((1,), (0,)), ((), ()))):
    (ah, al), (bh, bl) = a, b
    d = functools.partial(lax.dot_general, dimension_numbers=dims, preferred_element_type=F32)
    return d(ah, bh) + (d(ah, bl) + d(al, bh))


def kernel(pid, hist_hbm, ridge, pinv_hbm, fa_hbm, fb_hbm,
           hist, pT, msk, cor, comb, yin, mid, xin,
           q2z, s2z, qdz, sdz, qaz, saz, qxz, sxz,
           q2x, s2x, qdx, sdx, qax, sax, qxx, sxx,
           r2z, t2z, rdz, tdz, raz, taz, rxz, txz,
           r2x, t2x, rdx, tdx, rax, tax, rxx, txx,
           keep, pvp, pvr, pvs, gram, cross, fa, fb, pinv, ahi, alo,
           bs, br, zs, zr, xs, xr, ps, pr, hs, qs, os):
    u = lax.axis_index("users")
    y = lax.axis_index("srow")
    s = lax.axis_index("scol")
    z, xl = u // 2, u % 2
    xh, co = s // 2, s % 2
    g = y * 4 + s
    users, items = hist.shape
    total_rows = float(users * 8)
    zc = items // 4
    half = zc // 2
    first_item = g * items + u * half
    bufs = {"Z": dict(q2=(q2z, s2z), qd=(qdz, sdz), qa=(qaz, saz), qx=(qxz, sxz),
                      r2=(r2z, t2z), rd=(rdz, tdz), ra=(raz, taz), rx=(rxz, txz)),
            "X": dict(q2=(q2x, s2x), qd=(qdx, sdx), qa=(qax, sax), qx=(qxx, sxx),
                      r2=(r2x, t2x), rd=(rdx, tdx), ra=(rax, tax), rx=(rxx, txx))}

    def at(z_=None, xl_=None, y_=None, xh_=None, co_=None):
        zz = z if z_ is None else z_
        ll = xl if xl_ is None else xl_
        yy = y if y_ is None else y_
        hh = xh if xh_ is None else xh_
        cc = co if co_ is None else co_
        return (zz * 2 + ll, yy, hh * 2 + cc)

    up, dn, op = (z + 1) % 4, (z + 3) % 4, (z + 2) % 4
    p_up, p_dn, p_x = at(z_=up), at(z_=dn), at(xl_=1 - xl)
    p_core, p_xh = at(co_=1 - co), at(xh_=1 - xh)
    p_y = [at(y_=(y + d) % 4) for d in (1, 2, 3)]
    p_u = [((u + d) % 8, y, s) for d in range(1, 8)]
    p_ux = [((u + d) % 8, y, (xh + b) % 2 * 2 + co) for d in range(8) for b in range(2)][1:]

    load = pltpu.make_async_copy(hist_hbm, hist, hs)
    load.start()
    barrier = pltpu.get_barrier_semaphore()
    everyone = [p_core] + p_y + p_ux
    for peer in everyone:
        pl.semaphore_signal(barrier, inc=1, device_id=peer, device_id_type=MESH)
    pl.semaphore_wait(barrier, len(everyone))
    load.wait()

    live, descs, waited = {}, {}, set()

    def send(key, src, dst, ss, rs, peer):
        c = pltpu.make_async_remote_copy(src, dst, ss, rs, device_id=peer, device_id_type=MESH)
        c.start()
        live[key] = descs[key] = c

    def got(key):
        live.pop(key).wait_recv()

    def wait_sent(key):
        if key in descs and key not in waited:
            waited.add(key)
            descs[key].wait_send()

    def sendq(key, src, dst, ss, rs, i, peer):
        for n in (0, 1):
            send(key + (n,), src[n], dst[n], ss.at[i + n], rs.at[i + n], peer)

    def gotq(key):
        for n in (0, 1):
            got(key + (n,))

    def sentq(key):
        for n in (0, 1):
            wait_sent(key + (n,))

    def bc1(c):
        k, j = divmod(c, HALF)
        v = None
        for b in range(items // 1024):
            mine = (pid[k] == 4 * g + b).astype(F32).astype(BF16)
            term = hist[:, pl.ds(b * 1024 + j * CW, CW)] * mine
            v = term if v is None else v + term
        wait_sent(("b0", c - 3))
        msk[c % 3] = v.T
        send(("b0", c), msk.at[c % 3, pl.ds(pl.multiple_of((1 - co) * 128, 128), 128)], cor.at[c], bs.at[c, 0], br.at[c, 0], p_core)

    def bc2(c):
        got(("b0", c))
        for d in (1, 2, 3):
            wait_sent(("b1", c - 3, d))
        comb[c % 3] = msk[c % 3, pl.ds(pl.multiple_of(co * 128, 128), 128)] + cor[c]
        for d in (1, 2, 3):
            yy = (y + d) % 4
            send(("b1", c, d), comb.at[c % 3, pl.ds(pl.multiple_of(yy * 32, 32), 32)], yin.at[c, d - 1],
                 bs.at[c, d], br.at[c, d], p_y[d - 1])

    def bc3(c):
        for d in (1, 2, 3):
            got(("b1", c, d))
        mid[c] = comb[c % 3, pl.ds(pl.multiple_of(y * 32, 32), 32)] + yin[c, 0] + yin[c, 1] + yin[c, 2]
        send(("b2", c), mid.at[c], xin.at[c], bs.at[c, 4], br.at[c, 4], p_xh)

    def bc4(c):
        got(("b2", c))
        here = pl.ds(pl.multiple_of(co * 128 + y * 32, 32), 32)
        pT[c, here] = mid[c] + xin[c]
        for d in (1, 2, 3):
            send(("b3", c, d), pT.at[c, here], pT.at[c, here], bs.at[c, 4 + d], br.at[c, 4 + d], p_y[d - 1])

    def bc5(c):
        for d in (1, 2, 3):
            got(("b3", c, d))
        here = pl.ds(pl.multiple_of(co * 128, 128), 128)
        send(("b4", c), pT.at[c, here], pT.at[c, here], bs.at[c, 8], br.at[c, 8], p_core)

    def bc6(c):
        got(("b4", c))

    def tiles(c, lane0, width, adds, out):
        def one(t, carry):
            lane = pl.multiple_of(lane0 + t * 256, 256)
            o = pl.multiple_of(t * 256, 256)
            v = jnp.dot(pT[c], hist[:, pl.ds(lane, 256)], preferred_element_type=F32)
            for q, sc in adds:
                v = v + decode(q[:, pl.ds(o, 256)], sc[:, pl.ds(o, 256)])
            out(o, v)
            return carry
        if width == 256:
            one(0, 0)
        else:
            lax.fori_loop(0, width // 256, one, 0)

    def coded(buf):
        def out(o, v):
            q, sc = encode(v)
            buf[0][:, pl.ds(o, 256)] = q
            buf[1][:, pl.ds(o, 256)] = sc
        return out

    def final(c):
        k, j = divmod(c, HALF)

        def out(o, v):
            r = lax.broadcasted_iota(jnp.int32, v.shape, 0) + (pid[k] * 1024 + j * CW)
            i = lax.broadcasted_iota(jnp.int32, v.shape, 1) + (first_item + o)
            v = v * (1.0 / total_rows) + jnp.where(r == i, ridge[:, pl.ds(o, 256)], 0.0)
            gram[c % HALF, pl.ds(o, 256)] = v.T
        return out

    def width(c):
        return half if KINDS[c] == "Z" else half // 2

    def pick(c, name, *ix):
        lead = NTH[c] % 2 if name[0] == "q" else NTH[c]
        return tuple(b.at[(lead,) + ix] for b in bufs[KINDS[c]][name])

    def before(c):
        n = NTH[c]
        return ORDER[KINDS[c]][n - 2] if n >= 2 else -1

    def lane(c, zz, h):
        if KINDS[c] == "Z":
            return zz * zc + h * half
        return zz * zc + xl * half + h * (half // 2)

    def xadd(c, i, h):
        if KINDS[c] == "Z":
            return []
        w = half // 2
        q, sc = pick(c, "rx", i)
        return [(q.at[:, pl.ds(h * w, w)], sc.at[:, pl.ds(h * w, w)])]

    def x1(c, some=(0, 1, 2, 3)):
        for i in some:
            zz = (op, up, dn, z)[i]
            sentq(("x", before(c), i))
            tiles(c, zz * zc + (1 - xl) * half, half, [], coded(pick(c, "qx", i)))
            sendq(("x", c, i), pick(c, "qx", i), pick(c, "rx", i), xs.at[c], xr.at[c], 2 * i, p_x)

    def step(c, name, dst, h, zz, i, adds, ss, peer):
        sentq((name, before(c), h))
        tiles(c, lane(c, zz, h), width(c), xadd(c, i, h) + adds, coded(pick(c, name, h)))
        sendq((name, c, h), pick(c, name, h), pick(c, dst, h), zs.at[c], zr.at[c], ss + 2 * h, peer)

    def z_first(c):
        if KINDS[c] == "X":
            gotq(("x", c, 0))
        for h, peer in ((0, p_dn), (1, p_up)):
            step(c, "q2", "r2", h, op, 0, [], 0, peer)

    def z_direct(c):
        if KINDS[c] == "X":
            gotq(("x", c, 1))
            gotq(("x", c, 2))
        for h, zz, i, peer in ((0, up, 1, p_up), (1, dn, 2, p_dn)):
            step(c, "qd", "rd", h, zz, i, [], 4, peer)

    def z_pass(c):
        for h, zz, i, peer in ((0, dn, 2, p_dn), (1, up, 1, p_up)):
            gotq(("q2", c, h))
            step(c, "qa", "ra", h, zz, i, [pick(c, "r2", h)], 8, peer)

    def z_last(c):
        if KINDS[c] == "X":
            gotq(("x", c, 3))
        for h in (0, 1):
            gotq(("qd", c, h))
            gotq(("qa", c, h))
        if KINDS[c] == "X":
            for h in (0, 1):
                def out(o, v, h=h):
                    final(c)(h * width(c) + o, v)
                tiles(c, lane(c, z, h), width(c), xadd(c, 3, h) + [pick(c, "rd", h), pick(c, "ra", h)], out)
            return
        sentq(("x", before(c), 0))
        tiles(c, lane(c, z, 1 - xl), half, [pick(c, "rd", 1 - xl), pick(c, "ra", 1 - xl)], coded(pick(c, "qx")))
        sendq(("x", c, 0), pick(c, "qx"), pick(c, "rx"), xs.at[c], xr.at[c], 0, p_x)

        def out(o, v):
            keep[NTH[c] % 2, :, pl.ds(o, 256)] = v
        tiles(c, lane(c, z, xl), half, [pick(c, "rd", xl), pick(c, "ra", xl)], out)

    def x_last(c):
        gotq(("x", c, 0))
        q, sc = pick(c, "rx")

        def one(t, carry):
            o = pl.multiple_of(t * 256, 256)
            final(c)(o, keep[NTH[c] % 2, :, pl.ds(o, 256)] + decode(q[:, pl.ds(o, 256)], sc[:, pl.ds(o, 256)]))
            return carry
        lax.fori_loop(0, half // 256, one, 0)

    def pv1():
        rows = pT[HALF + g // 4, pl.ds(pl.multiple_of((g % 4) * 64, 64), 64)]
        for j in range(HALF):
            pvp[:, pl.ds(j * CW, CW)] = lax.dot_general(
                rows, pT[j], (((1,), (1,)), ((), ())), preferred_element_type=F32)
        for d in range(1, 8):
            uu = (u + d) % 8
            send(("p0", d), pvp.at[pl.ds(pl.multiple_of(uu * 8, 8), 8)], pvr.at[d - 1], ps.at[d - 1], pr.at[d - 1], p_u[d - 1])

    def pv2():
        v = pvp[pl.ds(pl.multiple_of(u * 8, 8), 8)]
        for d in range(1, 8):
            got(("p0", d))
            v = v + pvr[d - 1]
        here = pl.ds(pl.multiple_of(u * 8, 8), 8)
        pvs[g, here] = v * (1.0 / total_rows)
        for d, peer in enumerate(p_ux):
            send(("p1", d), pvs.at[g, here], pvs.at[g, here], ps.at[7 + d], pr.at[7 + d], peer)

    def pv3():
        for d in range(15):
            got(("p1", d))
        for d in (1, 2, 3):
            for b in (0, 1):
                gg = y * 4 + b * 2 + co
                send(("p2", d, b), pvs.at[gg], pvs.at[gg], ps.at[20 + 2 * d + b], pr.at[20 + 2 * d + b], p_y[d - 1])

    def pv4():
        for d in (1, 2, 3):
            for b in (0, 1):
                got(("p2", d, b))
        for b in range(8):
            gg = b * 2 + co
            send(("p3", b), pvs.at[gg], pvs.at[gg], ps.at[28 + b], pr.at[28 + b], p_core)

    def pv5():
        for b in range(8):
            got(("p3", b))

    def fetch(c):
        k, j = divmod(c, HALF)
        return pltpu.make_async_copy(pinv_hbm.at[k, pl.ds(j * CW, CW)], pinv.at[c % 2], qs.at[c % 2])

    def factor(c):
        k, j = divmod(c, HALF)
        acc = (fa, fb)[k]
        d = gram[j] if k == 0 else gram[j] - cross[j]
        hi, lo = split(d)
        ahi[:, pl.ds(0, CW)] = hi
        alo[:, pl.ds(0, CW)] = lo
        fetch(c).wait()

        def one(t, carry):
            here = pl.ds(pl.multiple_of(t * 256, 256), 256)
            v = dot3((ahi[:, pl.ds(0, CW)], alo[:, pl.ds(0, CW)]), split(pinv[c % 2, :, here]))
            acc[:, here] = v if j == 0 else acc[:, here] + v
            return carry
        lax.fori_loop(0, 4, one, 0)
        if c + 2 < NCH:
            fetch(c + 2).start()

    def out_copy(k):
        return pltpu.make_async_copy((fa, fb)[k], (fa_hbm, fb_hbm)[k], os.at[k])

    def crossing():
        out_copy(0).start()

        def part(t, carry):
            here = pl.ds(pl.multiple_of(t * 256, 256), 256)
            hi, lo = split(fa[:, here])
            ahi[:, here] = hi
            alo[:, here] = lo
            return carry
        lax.fori_loop(0, 4, part, 0)

        def one(t, carry):
            rows = pvs[pl.ds(t * 4, 4)].reshape(256, 1024)
            cross[t] = dot3((ahi[...], alo[...]), split(rows), (((1,), (1,)), ((), ())))
            return carry
        lax.fori_loop(0, 4, one, 0)

    fetch(0).start()
    fetch(1).start()

    bc = (bc1, bc2, bc3, bc4, bc5, bc6)

    def slot(t):
        for n in reversed(range(6)):
            if 0 <= t - n < NCH:
                bc[n](t - n)

    for t in range(6):
        slot(t)
    slots = list(range(6, NCH + 5))
    pvq = [pv1, pv2, pv3, pv4, pv5]
    stages = {"Z": ((z_first, z_direct), (z_pass,), (z_last,), (x_last,)),
              "X": ((x1,), (z_first, z_direct), (z_pass,), (z_last,))}
    done = 0
    for i in range(NCH + 3):
        for lag in range(4):
            c = i - lag
            if not 0 <= c < NCH:
                continue
            for f in stages[KINDS[c]][lag]:
                f(c)
                if slots:
                    slot(slots.pop(0))
            if lag == 3 and c < HALF:
                factor(c)
        if not slots and pvq:
            pvq.pop(0)()
        if i == NCH:
            while pvq:
                pvq.pop(0)()
            crossing()
        if i >= NCH:
            while done < HALF and HALF + done + 3 <= i:
                factor(HALF + done)
                done += 1
    out_copy(1).start()
    for key in descs:
        wait_sent(key)
    out_copy(0).wait()
    out_copy(1).wait()


def run(history, ridge, pivot_inverse, panel_ids):
    users, items = history.shape
    half = items // 8
    vm = pltpu.VMEM
    dma = pltpu.SemaphoreType.DMA
    nz, nx = len(ORDER["Z"]), len(ORDER["X"])
    scratch = [
        vm((users, items), BF16), vm((NCH, CW, users), BF16), vm((3, CW, users), BF16),
        vm((NCH, 128, users), BF16), vm((3, 128, users), BF16), vm((NCH, 3, 32, users), BF16),
        vm((NCH, 32, users), BF16), vm((NCH, 32, users), BF16),
    ]
    for lead, w in (((2, 2), half), ((2, 2), half), ((2, 2), half), ((2,), half),
                    ((2, 2), half // 2), ((2, 2), half // 2), ((2, 2), half // 2), ((2, 4), half),
                    ((nz, 2), half), ((nz, 2), half), ((nz, 2), half), ((nz,), half),
                    ((nx, 2), half // 2), ((nx, 2), half // 2), ((nx, 2), half // 2), ((nx, 4), half)):
        scratch += [vm(lead + (CW, w), I16), vm(lead + (1, w), F32)]
    scratch += [
        vm((2, CW, half), F32),
        vm((64, 1024), F32), vm((7, 8, 1024), F32), vm((16, 64, 1024), F32),
        vm((HALF, half, CW), F32), vm((HALF, half, CW), F32),
        vm((half, 1024), F32), vm((half, 1024), F32), vm((2, CW, 1024), F32),
        vm((half, 1024), BF16), vm((half, 1024), BF16),
        dma((NCH, 9)), dma((NCH, 9)), dma((NCH, 12)), dma((NCH, 12)), dma((NCH, 8)), dma((NCH, 8)),
        dma((36,)), dma((36,)), dma, dma((2,)), dma((2,)),
    ]
    hbm = pl.BlockSpec(memory_space=pl.ANY)
    return pl.pallas_call(
        kernel,
        out_shape=(jax.ShapeDtypeStruct((half, 1024), F32),) * 2,
        in_specs=[pl.BlockSpec(memory_space=pltpu.SMEM), hbm, pl.BlockSpec(memory_space=pltpu.VMEM), hbm],
        out_specs=(hbm, hbm),
        scratch_shapes=scratch,
        compiler_params=pltpu.CompilerParams(collective_id=1, has_side_effects=True, vmem_limit_bytes=62 * 2**20),
    )(panel_ids, history, ridge, pivot_inverse)


def local(history, ridge, pivot_inverse, panel_ids):
    group_items = history.shape[1]
    block_rows = group_items // 8
    first_row = lax.axis_index(("srow", "scol")) * group_items + lax.axis_index("users") * block_rows
    ridge_here = lax.dynamic_slice_in_dim(ridge, first_row, block_rows)
    factor_a, factor_b = run(history, ridge_here[None], pivot_inverse, panel_ids)
    return factor_a[None], factor_b[None]


def solution(mesh):
    return jax.shard_map(
        local,
        mesh=mesh,
        in_specs=(P("users", ("srow", "scol")), P(), P(), P()),
        out_specs=(P(("srow", "scol"), "users", None), P(("srow", "scol"), "users", None)),
        check_vma=False,
    )
```

profile of v0, /device:TPU:0, one launch (start us, length us, event | category | flops | bytes accessed | tf_op | source)
XLA Modules:
  0.0 191.3 jit_solution(11513120786786455031)
XLA Ops:
  0.6 1.3 dynamic_slice.3
  2.0 184.7 %shard_map.59 = (f32[512,1024]{1,0:T(8,128)}, f32[512,1024]{1,0:T(8,128)}) custom-call(s32[2]{0:T(128)} %pid.1, bf16[1024,4096]{1,0:T(8,128)(2,1)} %hist_hbm.1, f32[1,512]{1,0:T(1,128)} %bitcast.5, f32[2,1024,1024]{2,1,0:T(8,128)} %pinv_hbm.1), custom_call_target="tpu_custom_call" | custom-call | tf_op jit(solution)/shard_map/pallas_call | solution.py:429
  186.7 0.0 copy-start
  186.7 3.3 %copy.8 = f32[1,512,1024]{2,1,0:T(8,128)} copy(f32[1,512,1024]{2,1,0:T(8,128)} %bitcast.4) | data formatting | bytes 4194304
  190.0 0.0 copy-done
  190.0 1.3 copy.9
Async XLA Ops:
  186.7 3.3 %copy-start = (f32[512,1024]{1,0:T(8,128)S(1)}, f32[512,1024]{1,0:T(8,128)}, u32[]{:S(2)}) copy-start(f32[512,1024]{1,0:T(8,128)} %get-tuple-element.5) | copy-start | bytes 6291460
where the time goes:
time: 191 us
  Pallas kernels  185 us (97%)
  local copies, waits for them, and re-layouts  5.97 us (3%)
    pallas_call x1, Pallas kernels, run(): pl.pallas_call(kernel, out_shape=(jax.ShapeDtypeStruct((half, 1024), F32)...  185 us
    unnamed x4, local copies, waits for them, and re-layouts  4.63 us

commit v1 on v0

--- a/solution.py
+++ b/solution.py
@@ -131,17 +131,17 @@
     def bc2(c):
         got(("b0", c))
         for d in (1, 2, 3):
-            wait_sent(("b1", c - 3, d))
-        comb[c % 3] = msk[c % 3, pl.ds(pl.multiple_of(co * 128, 128), 128)] + cor[c]
+            wait_sent(("b1", c - NCH, d))
+        comb[c] = msk[c % 3, pl.ds(pl.multiple_of(co * 128, 128), 128)] + cor[c]
         for d in (1, 2, 3):
             yy = (y + d) % 4
-            send(("b1", c, d), comb.at[c % 3, pl.ds(pl.multiple_of(yy * 32, 32), 32)], yin.at[c, d - 1],
+            send(("b1", c, d), comb.at[c, pl.ds(pl.multiple_of(yy * 32, 32), 32)], yin.at[c, d - 1],
                  bs.at[c, d], br.at[c, d], p_y[d - 1])
 
     def bc3(c):
         for d in (1, 2, 3):
             got(("b1", c, d))
-        mid[c] = comb[c % 3, pl.ds(pl.multiple_of(y * 32, 32), 32)] + yin[c, 0] + yin[c, 1] + yin[c, 2]
+        mid[c] = comb[c, pl.ds(pl.multiple_of(y * 32, 32), 32)] + yin[c, 0] + yin[c, 1] + yin[c, 2]
         send(("b2", c), mid.at[c], xin.at[c], bs.at[c, 4], br.at[c, 4], p_xh)
 
     def bc4(c):
@@ -358,32 +358,51 @@
     fetch(0).start()
     fetch(1).start()
 
-    bc = (bc1, bc2, bc3, bc4, bc5, bc6)
-
-    def slot(t):
-        for n in reversed(range(6)):
-            if 0 <= t - n < NCH:
-                bc[n](t - n)
-
-    for t in range(6):
-        slot(t)
-    slots = list(range(6, NCH + 5))
+    bc1(0)
+    for c in range(1, NCH):
+        bc1(c)
+        bc2(c - 1)
+    bc2(NCH - 1)
+    bc3(0)
+    for c in range(1, NCH):
+        bc3(c)
+        bc4(c - 1)
+    bc4(NCH - 1)
+    arrive = [functools.partial(bc5, c) for c in range(2)]
+    for c in range(NCH):
+        arrive.append(functools.partial(bc6, c))
+        if c + 2 < NCH:
+            arrive.append(functools.partial(bc5, c + 2))
+
+    def until(c):
+        while arrive and arrive[0].args[0] <= c + 2:
+            f = arrive.pop(0)
+            f()
+            if f.func is bc6 and f.args[0] == c:
+                break
+
     pvq = [pv1, pv2, pv3, pv4, pv5]
     stages = {"Z": ((z_first, z_direct), (z_pass,), (z_last,), (x_last,)),
               "X": ((x1,), (z_first, z_direct), (z_pass,), (z_last,))}
     done = 0
     for i in range(NCH + 3):
+        if any(f.func is bc6 and f.args[0] == i for f in arrive):
+            until(i)
         for lag in range(4):
             c = i - lag
             if not 0 <= c < NCH:
                 continue
             for f in stages[KINDS[c]][lag]:
                 f(c)
-                if slots:
-                    slot(slots.pop(0))
+                if arrive:
+                    arrive.pop(0)()
+                if arrive:
+                    arrive.pop(0)()
             if lag == 3 and c < HALF:
                 factor(c)
-        if not slots and pvq:
+        if i in (2, 4, 5, 7):
+            while arrive:
+                arrive.pop(0)()
             pvq.pop(0)()
         if i == NCH:
             while pvq:
@@ -408,7 +427,7 @@
     nz, nx = len(ORDER["Z"]), len(ORDER["X"])
     scratch = [
         vm((users, items), BF16), vm((NCH, CW, users), BF16), vm((3, CW, users), BF16),
-        vm((NCH, 128, users), BF16), vm((3, 128, users), BF16), vm((NCH, 3, 32, users), BF16),
+        vm((NCH, 128, users), BF16), vm((NCH, 128, users), BF16), vm((NCH, 3, 32, users), BF16),
         vm((NCH, 32, users), BF16), vm((NCH, 32, users), BF16),
     ]
     for lead, w in (((2, 2), half), ((2, 2), half), ((2, 2), half), ((2,), half),

time: 191 us -> 188 us (0.984)
  Pallas kernels: 185 us -> 181 us
    pallas_call x1, Pallas kernels: 185 us -> 181 us  [run(): pl.pallas_call(kernel, out_shape=(jax.ShapeDtypeStruct((half, 1024), F32)...]
where the time goes in v1:
time: 188 us
  Pallas kernels  181 us (96%)
  local copies, waits for them, and re-layouts  5.97 us (3%)
    pallas_call x1, Pallas kernels, run(): pl.pallas_call(kernel, out_shape=(jax.ShapeDtypeStruct((half, 1024), F32)...  181 us
    unnamed x4, local copies, waits for them, and re-layouts  4.63 us

profile of v1, /device:TPU:0, one launch (start us, length us, event | category | flops | bytes accessed | tf_op | source)
XLA Modules:
  0.0 187.9 jit_solution(16854007647658983576)
XLA Ops:
  0.6 1.3 dynamic_slice.3
  2.0 181.2 %shard_map.59 = (f32[512,1024]{1,0:T(8,128)}, f32[512,1024]{1,0:T(8,128)}) custom-call(s32[2]{0:T(128)} %pid.1, bf16[1024,4096]{1,0:T(8,128)(2,1)} %hist_hbm.1, f32[1,512]{1,0:T(1,128)} %bitcast.5, f32[2,1024,1024]{2,1,0:T(8,128)} %pinv_hbm.1), custom_call_target="tpu_custom_call" | custom-call | tf_op jit(solution)/shard_map/pallas_call | solution.py:448
  183.2 0.0 copy-start
  183.2 3.3 %copy.8 = f32[1,512,1024]{2,1,0:T(8,128)} copy(f32[1,512,1024]{2,1,0:T(8,128)} %bitcast.4) | data formatting | bytes 4194304
  186.5 0.0 copy-done
  186.5 1.3 copy.9
Async XLA Ops:
  183.2 3.3 %copy-start = (f32[512,1024]{1,0:T(8,128)S(1)}, f32[512,1024]{1,0:T(8,128)}, u32[]{:S(2)}) copy-start(f32[512,1024]{1,0:T(8,128)} %get-tuple-element.5) | copy-start | bytes 6291460
